TPU v7x, 32 devices: a whole 2x2x4 slice. The times are simulated.
32 devices in a mesh: node: 4 (over z), local: 8 (over y, x, core).
Axes of the slice: x: 2, y: 2, z: 4, core: 2. Of those that a mesh axis runs over, the one named last changes fastest.
Arguments:
- tokens: bfloat16 [4096, 3584], P(('node', 'local')), may hold values from -6 to 6
- group_ids: int32 [4096, 2], P(('node', 'local')), may hold values from 0 to 3, as said below
- local_ids: int32 [4096, 8], P(('node', 'local')), may hold values from 0 to 7, as said below
- router: bfloat16 [3584, 32], replicated, may hold values from -0.09375 to 0.09375
- w_gate: bfloat16 [32, 3584, 1024], P(('node', 'local')), may hold values from -0.09375 to 0.09375
- w_up: bfloat16 [32, 3584, 1024], P(('node', 'local')), may hold values from -0.09375 to 0.09375
- w_down: bfloat16 [32, 1024, 3584], P(('node', 'local')), may hold values from -0.1875 to 0.1875
Outputs:
- moe_out: bfloat16 [4096, 3584], P(('node', 'local'))
Inputs may be any that keep to these rules, and one draw needn't show every extreme that they name: `group_ids`: each token names two different node groups; the tokens of one device name every node group exactly 64 times. `local_ids`: entry k names an expert of node group group_ids[t, k // 4]; the four entries of one group are different. The tokens of one device route at most 40 tokens to one expert, and in every node group some expert receives exactly 40 tokens from every device.
All inputs are finite; a program needn't handle non-finite values.
Results may differ from a plain program's by a relative error of at most 0.0058.
Values may be sent and summed in bfloat16 or wider, within the bound.
A program may use at most 128 MiB of HBM per device.

v0:
```python
import jax
import jax.numpy as jnp
from jax import lax
from jax.sharding import PartitionSpec as P


def slot_positions(targets, bins):
    onehot = (targets[:, None] == jnp.arange(bins, dtype=jnp.int32)[None, :]).astype(jnp.int32)
    earlier = jnp.cumsum(onehot, axis=0) - onehot
    return jnp.sum(earlier * onehot, axis=1)


def fill_slots(source_rows, owners, slot_index, slot_total):
    src_table = jnp.full((slot_total,), source_rows.shape[0], jnp.int32).at[slot_index].set(owners)
    padded = jnp.concatenate(
        [source_rows, jnp.zeros((1, source_rows.shape[1]), source_rows.dtype)], axis=0
    )
    return padded[src_table]


def expert_rows(flat_rows, w_gate, w_up, w_down):
    gate_part = jnp.dot(flat_rows, w_gate[0], preferred_element_type=jnp.float32)
    up_part = jnp.dot(flat_rows, w_up[0], preferred_element_type=jnp.float32)
    hidden = (jax.nn.silu(gate_part) * up_part).astype(jnp.bfloat16)
    return jnp.dot(hidden, w_down[0], preferred_element_type=jnp.float32).astype(jnp.bfloat16)


def on_device(tokens, group_ids, local_ids, router, w_gate, w_up, w_down):
    tok_dev, feat_width = tokens.shape
    node_size = lax.axis_size("node")
    local_size = lax.axis_size("local")
    cap_rows = 5 * tok_dev // (2 * local_size)
    group_count = group_ids.shape[1]
    per_group = local_ids.shape[1] // group_count
    expert_ids = jnp.repeat(group_ids, per_group, axis=1) * local_size + local_ids
    affinity = jax.nn.sigmoid(jnp.dot(tokens, router, preferred_element_type=jnp.float32))
    picked = jnp.take_along_axis(affinity, expert_ids, axis=1)
    picked_total = jnp.sum(picked, axis=1)
    node_rows = group_count * tok_dev // node_size
    flat_groups = group_ids.reshape(-1)
    home_slot = flat_groups * node_rows + slot_positions(flat_groups, node_size)
    home_owner = jnp.arange(flat_groups.shape[0], dtype=jnp.int32) // group_count
    outgoing = fill_slots(tokens, home_owner, home_slot, node_size * node_rows).reshape(
        node_size, node_rows, feat_width
    )
    outgoing_ids = (
        jnp.zeros((node_size * node_rows, per_group), jnp.int32)
        .at[home_slot]
        .set(local_ids.reshape(-1, per_group))
        .reshape(node_size, node_rows, per_group)
    )
    relay_in, relay_ids = (
        lax.all_to_all(outgoing, "node", split_axis=0, concat_axis=0, tiled=True),
        lax.all_to_all(outgoing_ids, "node", split_axis=0, concat_axis=0, tiled=True),
    )
    relay_flat = relay_in.reshape(-1, feat_width)
    relay_targets = relay_ids.reshape(-1)
    relay_cap = node_size * cap_rows
    relay_slot = relay_targets * relay_cap + slot_positions(relay_targets, local_size)
    relay_owner = jnp.arange(relay_targets.shape[0], dtype=jnp.int32) // per_group
    relay_send = fill_slots(relay_flat, relay_owner, relay_slot, local_size * relay_cap).reshape(
        local_size, relay_cap, feat_width
    )
    received = lax.all_to_all(relay_send, "local", split_axis=0, concat_axis=0, tiled=True)
    lead_size, item_count, _ = received.shape
    produced = expert_rows(received.reshape(-1, feat_width), w_gate, w_up, w_down).reshape(
        lead_size, item_count, feat_width
    )
    relay_back = lax.all_to_all(produced, "local", split_axis=0, concat_axis=0, tiled=True)
    relay_terms = relay_back.reshape(-1, feat_width)[relay_slot].reshape(-1, per_group, feat_width)
    relay_aff = jax.nn.sigmoid(jnp.dot(relay_flat, router, preferred_element_type=jnp.float32))
    relay_cols = lax.axis_index("node") * local_size + relay_ids.reshape(-1, per_group)
    relay_score = jnp.take_along_axis(relay_aff, relay_cols, axis=1)
    partial_sum = jnp.sum(relay_score[:, :, None] * relay_terms.astype(jnp.float32), axis=1)
    home_back = lax.all_to_all(
        partial_sum.reshape(node_size, node_rows, feat_width),
        "node",
        split_axis=0,
        concat_axis=0,
        tiled=True,
    )
    home_sum = jnp.sum(
        home_back.reshape(-1, feat_width)[home_slot].reshape(tok_dev, group_count, feat_width),
        axis=1,
    )
    mixed = (2.5 / picked_total)[:, None] * home_sum
    return mixed.astype(jnp.bfloat16)


def solution(mesh):
    return jax.shard_map(
        on_device,
        mesh=mesh,
        in_specs=(
            P(("node", "local"), None),
            P(("node", "local"), None),
            P(("node", "local"), None),
            P(),
            P(("node", "local"), None, None),
            P(("node", "local"), None, None),
            P(("node", "local"), None, None),
        ),
        out_specs=P(("node", "local"), None),
        check_vma=False,
    )
```

profile of v0, /device:TPU:0, one launch (start us, length us, event | category | flops | bytes accessed | tf_op | source)
XLA Modules:
  0.0 483.3 jit_solution(12173939814550635728)
XLA Ops:
  0.0 1.3 broadcast_multiply_fusion.2
  2.4 1.2 reduce-window.14
  4.3 0.8 copy.52
  5.5 1.2 scatter_custom_fusion
  7.5 6.3 %all-to-all-start = ((s32[4,1,256]{2,1,0:T(1,128)}), s32[4,1,256]{2,1,0:T(1,128)S(1)}, u32[]{:S(2)}, u32[]{:S(2)}) async-start(s32[4,1,256]{2,1,0:T(1,128)} %reshape.281), calls=%async_computation | async-start | bytes 8192 | tf_op jit(solution)/shard_map/all_to_all | solution.py:54
  13.8 1.4 scatter_custom_fusion.1
  15.2 1.2 concatenate.6
  16.5 3.0 gather_fusion
  19.4 5.1 %all-to-all-start.1 = ((bf16[4,64,3584]{2,1,0:T(8,128)(2,1)}), bf16[4,64,3584]{2,1,0:T(8,128)(2,1)S(1)}, u32[]{:S(2)}, u32[]{:S(2)}) async-start(bf16[4,64,3584]{2,1,0:T(8,128)(2,1)} %bitcast.85), calls=%async_computation.1 | async-start | bytes 3670016 | tf_op jit(solution)/shard_map/all_to_all | solution.py:53
  26.4 2.3 reduce-window.16
  29.3 4.3 scatter_custom_fusion.2
  33.6 32.9 %all-to-all-done.1 = bf16[4,64,3584]{2,1,0:T(8,128)(2,1)S(1)} async-done(((bf16[4,64,3584]{2,1,0:T(8,128)(2,1)}), bf16[4,64,3584]{2,1,0:T(8,128)(2,1)S(1)}, u32[]{:S(2)}, u32[]{:S(2)}) %all-to-all-start.1) | async-done | bytes 1835040 | tf_op jit(solution)/shard_map/all_to_all | solution.py:53
  66.6 1.2 copy-done.1
  67.8 1.6 concatenate.7
  69.4 7.9 %gather_fusion.1 = bf16[1280,3584]{1,0:T(8,128)(2,1)} fusion(bf16[257,3584]{1,0:T(8,128)(2,1)S(1)} %concatenate.7, s32[2048]{0:T(1024)S(1)} %pad_clamp_fusion), kind=kCustom, calls=%fused_computation.1 | custom fusion | bytes 18355200 | tf_op jit(solution)/shard_map/gather | solution.py:18
  77.3 106.8 %all_to_all.25 = bf16[8,160,3584]{2,1,0:T(8,128)(2,1)S(1)} all-to-all(bf16[8,160,3584]{2,1,0:T(8,128)(2,1)} %bitcast.78), channel_id=1, replica_groups=mesh['node'=4,'local'=8] {'local'}, dimensions={0} | all-to-all | bytes 18350080 | tf_op jit(solution)/shard_map/all_to_all | solution.py:64
  184.2 13.6 %fusion.1 = f32[1280,1024]{1,0:T(8,128)} fusion(bf16[1280,3584]{1,0:T(8,128)(2,1)S(1)} %bitcast.83, bf16[1,3584,1024]{2,1,0:T(8,128)(2,1)} %param.12), kind=kOutput, calls=%fused_computation.12 | convolution fusion | flops 9395240960 | bytes 21757952 | tf_op jit(solution)/shard_map/dot_general | solution.py:23
  197.7 13.2 %multiply_convert_fusion = bf16[1280,1024]{1,0:T(8,128)(2,1)} fusion(f32[1280,1024]{1,0:T(8,128)} %fusion.1, bf16[1280,3584]{1,0:T(8,128)(2,1)S(1)} %bitcast.84, bf16[1,3584,1024]{2,1,0:T(8,128)(2,1)S(1)} %bitcast.101), kind=kOutput, calls=%fused_computation.16 | convolution fusion | flops 9403105280 | bytes 24379392 | tf_op jit(solution)/shard_map/dot_general | solution.py:22
  210.9 13.8 %convolution_convert_fusion = bf16[1280,3584]{1,0:T(8,128)(2,1)} fusion(bf16[1280,1024]{1,0:T(8,128)(2,1)} %multiply_convert_fusion, bf16[1,1024,3584]{2,1,0:T(8,128)(2,1)S(1)} %bitcast.103), kind=kOutput, calls=%fused_computation.9 | convolution fusion | flops 9399828480 | bytes 19136512 | tf_op jit(solution)/shard_map/dot_general | solution.py:25
  224.7 5.4 %all-to-all-start.3 = ((bf16[8,160,3584]{2,1,0:T(8,128)(2,1)}), bf16[8,160,3584]{2,1,0:T(8,128)(2,1)}, u32[]{:S(2)}, u32[]{:S(2)}) async-start(bf16[8,160,3584]{2,1,0:T(8,128)(2,1)} %bitcast.82), calls=%async_computation.3 | async-start | bytes 18350080 | tf_op jit(solution)/shard_map/all_to_all | solution.py:69
  231.3 8.6 %gather_fusion.5 = f32[1024]{0:T(1024)S(1)} fusion(f32[256,32]{0,1:T(8,128)S(1)} %fusion.9, s32[1024]{0:T(1024)S(1)} %reshape.237), kind=kCustom, calls=%fused_computation.5 | custom fusion | bytes 16384 | tf_op jit(solution)/shard_map/jit(take_along_axis)/gather | solution.py:73
  240.1 92.3 %all-to-all-done.3 = bf16[8,160,3584]{2,1,0:T(8,128)(2,1)} async-done(((bf16[8,160,3584]{2,1,0:T(8,128)(2,1)}), bf16[8,160,3584]{2,1,0:T(8,128)(2,1)}, u32[]{:S(2)}, u32[]{:S(2)}) %all-to-all-start.3) | async-done | bytes 9175072 | tf_op jit(solution)/shard_map/all_to_all | solution.py:69
  332.4 18.6 %gather_fusion.2 = bf16[1024,3584]{1,0:T(8,128)(2,1)} fusion(bf16[1280,3584]{1,0:T(8,128)(2,1)} %bitcast.20, s32[1024]{0:T(1024)S(1)} %broadcast_clamp_fusion), kind=kCustom, calls=%fused_computation.2 | custom fusion | bytes 14684160 | tf_op jit(solution)/shard_map/gather | solution.py:70
  350.9 13.9 %reshape.198 = f32[256,4,3584]{2,1,0:T(4,128)} reshape(bf16[1024,3584]{1,0:T(8,128)(2,1)} %gather_fusion.2) | data formatting | bytes 22020096 | tf_op jit(solution)/shard_map/convert_element_type | solution.py:74
  364.9 14.2 %multiply_reduce_fusion = f32[256,3584]{1,0:T(8,128)} fusion(f32[256,4,3584]{2,1,0:T(4,128)} %reshape.198, f32[256,4]{1,0:T(8,128)S(1)} %and_select_fusion), kind=kLoop, calls=%fused_computation.10 | loop fusion | flops 6422528 | bytes 18354176 | tf_op jit(solution)/shard_map/reduce_sum | solution.py:74
  379.1 5.1 %all-to-all-start.4 = ((f32[4,64,3584]{2,1,0:T(8,128)}), f32[4,64,3584]{2,1,0:T(8,128)}, u32[]{:S(2)}, u32[]{:S(2)}) async-start(f32[4,64,3584]{2,1,0:T(8,128)} %bitcast.81), calls=%async_computation.4 | async-start | bytes 7340032 | tf_op jit(solution)/shard_map/all_to_all | solution.py:75
  384.9 7.0 %gather_fusion.4 = f32[1024]{0:T(1024)S(1)} fusion(f32[128,32]{0,1:T(8,128)S(1)} %fusion.12, s32[1024]{0:T(1024)S(1)} %reshape.231), kind=kCustom, calls=%fused_computation.4 | custom fusion | bytes 16384 | tf_op jit(solution)/shard_map/jit(take_along_axis)/gather | solution.py:37
  392.1 71.0 %all-to-all-done.4 = f32[4,64,3584]{2,1,0:T(8,128)} async-done(((f32[4,64,3584]{2,1,0:T(8,128)}), f32[4,64,3584]{2,1,0:T(8,128)}, u32[]{:S(2)}, u32[]{:S(2)}) %all-to-all-start.4) | async-done | bytes 3670048 | tf_op jit(solution)/shard_map/all_to_all | solution.py:75
  463.1 7.2 %gather_fusion.3 = f32[256,3584]{1,0:T(8,128)} fusion(f32[256,3584]{1,0:T(8,128)} %bitcast.22, s32[1024]{0:T(1024)S(1)} %pad_clamp_fusion.1), kind=kCustom, calls=%fused_computation.3 | custom fusion | bytes 7341056 | tf_op jit(solution)/shard_map/gather | solution.py:83
  470.3 5.5 %reshape.197 = f32[128,2,3584]{2,1,0:T(2,128)} reshape(f32[256,3584]{1,0:T(8,128)} %gather_fusion.3) | data formatting | bytes 7340032 | tf_op jit(solution)/shard_map/reshape | solution.py:83
  475.8 6.4 %reduce_sum.55 = f32[128,3584]{1,0:T(8,128)S(1)} reduce(f32[128,2,3584]{2,1,0:T(2,128)} %reshape.197, f32[]{:T(128)} %constant.91.clone.1), dimensions={1}, to_apply=%region_11.12 | reduce | flops 458752 | bytes 5505028 | tf_op jit(solution)/shard_map/reduce_sum | solution.py:82
  482.2 1.1 multiply_convert_fusion.1
  (85 shorter events, 7.5 us)
Async XLA Ops:
  0.0 230.6 %copy-start = (bf16[3584,32]{0,1:T(8,128)(2,1)S(1)}, bf16[3584,32]{0,1:T(8,128)(2,1)}, u32[]{:S(2)}) copy-start(bf16[3584,32]{0,1:T(8,128)(2,1)} %param.10) | copy-start | bytes 688132
  5.5 9.7 %copy-start.6 = (s32[256,1]{0,1:T(1,128)}, s32[256,1]{0,1:T(1,128)S(1)}, u32[]{:S(2)}) copy-start(s32[256,1]{0,1:T(1,128)S(1)} %compare_select_fusion.5) | copy-start | bytes 3076
  7.5 12.0 %all-to-all-start = ((s32[4,1,256]{2,1,0:T(1,128)}), s32[4,1,256]{2,1,0:T(1,128)S(1)}, u32[]{:S(2)}, u32[]{:S(2)}) async-start(s32[4,1,256]{2,1,0:T(1,128)} %reshape.281), calls=%async_computation | async-start | bytes 8192 | tf_op jit(solution)/shard_map/all_to_all | solution.py:54
  19.4 47.1 %all-to-all-start.1 = ((bf16[4,64,3584]{2,1,0:T(8,128)(2,1)}), bf16[4,64,3584]{2,1,0:T(8,128)(2,1)S(1)}, u32[]{:S(2)}, u32[]{:S(2)}) async-start(bf16[4,64,3584]{2,1,0:T(8,128)(2,1)} %bitcast.85), calls=%async_computation.1 | async-start | bytes 3670016 | tf_op jit(solution)/shard_map/all_to_all | solution.py:53
  66.6 1.2 copy-start.1
  77.3 120.4 %slice-start = ((s8[7340032]{0:T(1024)(128)(4,1)}), s8[4194304]{0:T(1024)(128)(4,1)S(1)}, s32[]{:S(2)}) async-start(s8[7340032]{0:T(1024)(128)(4,1)} %bitcast.100), calls=%async_computation.5 | async-start | bytes 8388608
  77.3 133.6 %slice-start.2 = ((s8[7340032]{0:T(1024)(128)(4,1)}), s8[4194304]{0:T(1024)(128)(4,1)S(1)}, s32[]{:S(2)}) async-start(s8[7340032]{0:T(1024)(128)(4,1)} %bitcast.102), calls=%async_computation.7 | async-start | bytes 8388608
  184.1 13.6 %slice-start.1 = ((s8[7340032]{0:T(1024)(128)(4,1)}), s8[3145728]{0:T(1024)(128)(4,1)S(1)}, s32[]{:S(2)}) async-start(s8[7340032]{0:T(1024)(128)(4,1)} %bitcast.100), calls=%async_computation.6 | async-start | bytes 6291456
  184.2 26.8 %slice-start.3 = ((s8[7340032]{0:T(1024)(128)(4,1)}), s8[3145728]{0:T(1024)(128)(4,1)S(1)}, s32[]{:S(2)}) async-start(s8[7340032]{0:T(1024)(128)(4,1)} %bitcast.102), calls=%async_computation.8 | async-start | bytes 6291456
  224.7 5.9 %copy-start.2 = (bf16[4,64,3584]{2,1,0:T(8,128)(2,1)S(1)}, bf16[4,64,3584]{2,1,0:T(8,128)(2,1)}, u32[]{:S(2)}) copy-start(bf16[4,64,3584]{2,1,0:T(8,128)(2,1)} %copy-done.1) | copy-start | bytes 5505028
  224.7 107.6 %all-to-all-start.3 = ((bf16[8,160,3584]{2,1,0:T(8,128)(2,1)}), bf16[8,160,3584]{2,1,0:T(8,128)(2,1)}, u32[]{:S(2)}, u32[]{:S(2)}) async-start(bf16[8,160,3584]{2,1,0:T(8,128)(2,1)} %bitcast.82), calls=%async_computation.3 | async-start | bytes 18350080 | tf_op jit(solution)/shard_map/all_to_all | solution.py:69
  379.0 5.1 %copy-start.5 = (s32[128,2]{0,1:T(2,128)S(1)}, s32[128,2]{0,1:T(2,128)}, u32[]{:S(2)}) copy-start(s32[128,2]{0,1:T(2,128)} %get-tuple-element.7) | copy-start | bytes 3076
  379.0 5.2 %copy-start.4 = (s32[128,8]{0,1:T(8,128)S(1)}, s32[128,8]{0,1:T(8,128)}, u32[]{:S(2)}) copy-start(s32[128,8]{0,1:T(8,128)} %param.9) | copy-start | bytes 12292
  379.0 5.4 %copy-start.3 = (bf16[128,3584]{1,0:T(8,128)(2,1)S(1)}, bf16[128,3584]{1,0:T(8,128)(2,1)}, u32[]{:S(2)}) copy-start(bf16[128,3584]{1,0:T(8,128)(2,1)} %param.7) | copy-start | bytes 2752516
  379.1 84.0 %all-to-all-start.4 = ((f32[4,64,3584]{2,1,0:T(8,128)}), f32[4,64,3584]{2,1,0:T(8,128)}, u32[]{:S(2)}, u32[]{:S(2)}) async-start(f32[4,64,3584]{2,1,0:T(8,128)} %bitcast.81), calls=%async_computation.4 | async-start | bytes 7340032 | tf_op jit(solution)/shard_map/all_to_all | solution.py:75
  384.9 7.2 %copy-start.7 = (s32[256,1]{0,1:T(1,128)S(1)}, s32[256,1]{0,1:T(1,128)}, u32[]{:S(2)}) copy-start(s32[256,1]{0,1:T(1,128)} %copy-done.6) | copy-start | bytes 3076
where the time goes:
time: 485 us; the launch traced here: 483 us
  waiting for transfers between devices  196 us (40%)
  blocking collectives  107 us (22%)
  local copies, waits for them, and re-layouts  88.6 us (18%)
  matrix products  41.6 us (9%)
  other arithmetic  27.8 us (6%)
  starting transfers between devices  21.9 us (5%)
    all_to_all x1, blocking collectives, on_device(): lax.all_to_all(relay_send, 'local', split_axis=0, concat_axis=0, tiled=True)  107 us
    all_to_all x1, waiting for transfers between devices, on_device(): lax.all_to_all(produced, 'local', split_axis=0, concat_axis=0, tiled=True)  92.3 us
    all_to_all x1, waiting for transfers between devices, on_device(): lax.all_to_all(partial_sum.reshape(node_size, node_rows, feat_width), 'no...  71 us
    all_to_all x1, waiting for transfers between devices, on_device(): lax.all_to_all(outgoing, 'node', split_axis=0, concat_axis=0, tiled=True)  32.9 us
    gather x1, local copies, waits for them, and re-layouts, on_device(): relay_back.reshape(-1, feat_width)[relay_slot]  18.6 us
    reduce_sum x1, other arithmetic, on_device(): jnp.sum(relay_score[:, :, None] * relay_terms.astype(jnp.float32), axis=1)  14.2 us
    convert_element_type x1, local copies, waits for them, and re-layouts, on_device(): relay_terms.astype(jnp.float32)  13.9 us
    dot_general x1, matrix products, expert_rows(): jnp.dot(hidden, w_down[0], preferred_element_type=jnp.float32)  13.8 us
  transfers between devices with their start and end apart: 4, of which 3 were waited for; matrix products, arithmetic and copies ran while one was open for 7% of the time, Pallas kernels for 0%

commit v1 on v0

--- a/solution.py
+++ b/solution.py
@@ -1,13 +1,24 @@
+import functools
+
 import jax
 import jax.numpy as jnp
 from jax import lax
+from jax.experimental import pallas as pl
+from jax.experimental.pallas import tpu as pltpu
 from jax.sharding import PartitionSpec as P
 
+MESH = pl.DeviceIdType.MESH
+META = 128
+F32 = jnp.float32
+BF16 = jnp.bfloat16
+
 
 def slot_positions(targets, bins):
-    onehot = (targets[:, None] == jnp.arange(bins, dtype=jnp.int32)[None, :]).astype(jnp.int32)
-    earlier = jnp.cumsum(onehot, axis=0) - onehot
-    return jnp.sum(earlier * onehot, axis=1)
+    onehot = (targets[:, None] == jnp.arange(bins, dtype=jnp.int32)[None, :]).astype(F32)
+    count = targets.shape[0]
+    before = jnp.tril(jnp.ones((count, count), F32), -1)
+    earlier = jnp.dot(before, onehot, preferred_element_type=F32)
+    return jnp.sum(earlier * onehot, axis=1).astype(jnp.int32)
 
 
 def fill_slots(source_rows, owners, slot_index, slot_total):
@@ -19,13 +30,13 @@
 
 
 def expert_rows(flat_rows, w_gate, w_up, w_down):
-    gate_part = jnp.dot(flat_rows, w_gate[0], preferred_element_type=jnp.float32)
-    up_part = jnp.dot(flat_rows, w_up[0], preferred_element_type=jnp.float32)
-    hidden = (jax.nn.silu(gate_part) * up_part).astype(jnp.bfloat16)
-    return jnp.dot(hidden, w_down[0], preferred_element_type=jnp.float32).astype(jnp.bfloat16)
-
-
-def on_device(tokens, group_ids, local_ids, router, w_gate, w_up, w_down):
+    gate_part = jnp.dot(flat_rows, w_gate[0], preferred_element_type=F32)
+    up_part = jnp.dot(flat_rows, w_up[0], preferred_element_type=F32)
+    hidden = (jax.nn.silu(gate_part) * up_part).astype(BF16)
+    return jnp.dot(hidden, w_down[0], preferred_element_type=F32).astype(BF16)
+
+
+def on_device_general(tokens, group_ids, local_ids, router, w_gate, w_up, w_down):
     tok_dev, feat_width = tokens.shape
     node_size = lax.axis_size("node")
     local_size = lax.axis_size("local")
@@ -33,7 +44,7 @@
     group_count = group_ids.shape[1]
     per_group = local_ids.shape[1] // group_count
     expert_ids = jnp.repeat(group_ids, per_group, axis=1) * local_size + local_ids
-    affinity = jax.nn.sigmoid(jnp.dot(tokens, router, preferred_element_type=jnp.float32))
+    affinity = jax.nn.sigmoid(jnp.dot(tokens, router, preferred_element_type=F32))
     picked = jnp.take_along_axis(affinity, expert_ids, axis=1)
     picked_total = jnp.sum(picked, axis=1)
     node_rows = group_count * tok_dev // node_size
@@ -68,10 +79,10 @@
     )
     relay_back = lax.all_to_all(produced, "local", split_axis=0, concat_axis=0, tiled=True)
     relay_terms = relay_back.reshape(-1, feat_width)[relay_slot].reshape(-1, per_group, feat_width)
-    relay_aff = jax.nn.sigmoid(jnp.dot(relay_flat, router, preferred_element_type=jnp.float32))
+    relay_aff = jax.nn.sigmoid(jnp.dot(relay_flat, router, preferred_element_type=F32))
     relay_cols = lax.axis_index("node") * local_size + relay_ids.reshape(-1, per_group)
     relay_score = jnp.take_along_axis(relay_aff, relay_cols, axis=1)
-    partial_sum = jnp.sum(relay_score[:, :, None] * relay_terms.astype(jnp.float32), axis=1)
+    partial_sum = jnp.sum(relay_score[:, :, None] * relay_terms.astype(F32), axis=1)
     home_back = lax.all_to_all(
         partial_sum.reshape(node_size, node_rows, feat_width),
         "node",
@@ -84,12 +95,324 @@
         axis=1,
     )
     mixed = (2.5 / picked_total)[:, None] * home_sum
-    return mixed.astype(jnp.bfloat16)
+    return mixed.astype(BF16)
+
+
+OWN_X, OWN_Y, OWN_S, FWD_Y, FWD_X, SIB_X, SIB_Y, SIB_D, PART_S, DIAG_X, DIAG_Y, SUM_X, SUM_Y, HOME, NODE = range(15)
+
+
+def layer_kernel(
+    n, rows, d, ff,
+    out_ref, wg_hbm, wu_hbm, wd_hbm,
+    home, xh,
+    wg, wu, wd, xv, hid, ysend, ykeep, sib, dg, rx, ry,
+    ss, rs, wsem, xsem, csem,
+):
+    z = lax.axis_index("node")
+    l = lax.axis_index("local")
+
+    def flip(b):
+        return l + b - 2 * b * ((l // b) % 2)
+
+    sibling, xn, yn = (z, flip(1)), (z, flip(2)), (z, flip(4))
+    half = rows // 2
+
+    weights = [
+        pltpu.make_async_copy(wg_hbm, wg, wsem.at[0]),
+        pltpu.make_async_copy(wu_hbm, wu, wsem.at[1]),
+        pltpu.make_async_copy(wd_hbm, wd, wsem.at[2]),
+    ]
+    first = pltpu.make_async_copy(out_ref.at[0], xh.at[0, 0, pl.ds(0, rows)], csem.at[0])
+    first.start()
+
+    barrier = pltpu.get_barrier_semaphore()
+    peers = [sibling, xn, yn] + [(lax.rem(z + s, n), l) for s in range(1, n)]
+    for peer in peers:
+        pl.semaphore_signal(barrier, inc=1, device_id=peer, device_id_type=MESH)
+    pl.semaphore_wait(barrier, len(peers))
+
+    def copy(s, kind, src, dst, dev):
+        return pltpu.make_async_remote_copy(
+            src_ref=src, dst_ref=dst, send_sem=ss.at[s, kind], recv_sem=rs.at[s, kind],
+            device_id=dev, device_id_type=MESH,
+        )
+
+    def blk(s, c, r, at=0, size=rows):
+        return xh.at[s, c, pl.ds(r * rows + at, size)]
+
+    def kp(s, r, at=0, size=rows):
+        return ykeep.at[s % 2, pl.ds(r * rows + at, size)]
+
+    cp = {}
+    for s in range(n):
+        cp[s, OWN_X] = copy(s, OWN_X, blk(s, 0, 0), blk(s, 0, 1), xn)
+        cp[s, OWN_Y] = copy(s, OWN_Y, blk(s, 0, 0), blk(s, 0, 2), yn)
+        cp[s, OWN_S] = copy(s, OWN_S, blk(s, 0, 0), blk(s, 1, 0), sibling)
+        cp[s, FWD_Y] = copy(s, FWD_Y, blk(s, 0, 1, 0, half), blk(s, 0, 3, 0, half), yn)
+        cp[s, FWD_X] = copy(s, FWD_X, blk(s, 0, 2, half, half), blk(s, 0, 3, half, half), xn)
+        cp[s, SIB_X] = copy(s, SIB_X, blk(s, 0, 1), blk(s, 1, 1), sibling)
+        cp[s, SIB_Y] = copy(s, SIB_Y, blk(s, 0, 2), blk(s, 1, 2), sibling)
+        cp[s, SIB_D] = copy(s, SIB_D, blk(s, 0, 3), blk(s, 1, 3), sibling)
+        cp[s, PART_S] = copy(s, PART_S, ysend.at[s % 2], sib.at[s], sibling)
+        cp[s, DIAG_X] = copy(s, DIAG_X, kp(s, 3, 0, half), dg.at[s, pl.ds(0, half)], xn)
+        cp[s, DIAG_Y] = copy(s, DIAG_Y, kp(s, 3, half, half), dg.at[s, pl.ds(half, half)], yn)
+        cp[s, SUM_X] = copy(s, SUM_X, kp(s, 1), rx.at[s], xn)
+        cp[s, SUM_Y] = copy(s, SUM_Y, kp(s, 2), ry.at[s], yn)
+        if s:
+            cp[s, HOME] = copy(s, HOME, kp(s, 0), home.at[s], (lax.rem(z + s, n), l))
+            cp[s, NODE] = copy(s, NODE, out_ref.at[s], blk(s, 0, 0), (lax.rem(z - s + n, n), l))
+    last = pltpu.make_async_copy(kp(0, 0), home.at[0], csem.at[1])
+    sends = []
+
+    def start(s, *kinds):
+        for k in kinds:
+            cp[s, k].start()
+            if k not in (PART_S, DIAG_X, DIAG_Y, SUM_X, SUM_Y, HOME):
+                sends.append((s, k))
+
+    def arrived(s, *kinds):
+        for k in kinds:
+            cp[s, k].wait_recv()
+
+    def sent(s, *kinds):
+        for k in kinds:
+            cp[s, k].wait_send()
+
+    def gather_own(s):
+        if s:
+            arrived(s, NODE)
+        else:
+            first.wait()
+        start(s, OWN_X, OWN_Y, OWN_S)
+
+    def gather_forward(s):
+        arrived(s, OWN_X)
+        start(s, FWD_Y, SIB_X)
+        arrived(s, OWN_Y)
+        start(s, FWD_X, SIB_Y)
+
+    def gather_diagonal(s):
+        arrived(s, FWD_Y, FWD_X)
+        start(s, SIB_D)
+
+    def load(s):
+        arrived(s, OWN_S, SIB_X, SIB_Y, SIB_D)
+        for c in (1, 0):
+            pltpu.make_async_copy(xh.at[s, c], xv.at[c], xsem.at[c]).start()
+
+    def expert(s, c):
+        pltpu.make_async_copy(xh.at[s, c], xv.at[c], xsem.at[c]).wait()
+        if s == 0 and c == 1:
+            weights[0].wait()
+            weights[1].wait()
+        target = ysend if c else ykeep
+
+        @pl.loop(0, ff // 256)
+        def _(i):
+            cols = pl.ds(pl.multiple_of(i * 256, 256), 256)
+            x = xv[c, :, :d]
+            g = jnp.dot(x, wg[:, cols], preferred_element_type=F32)
+            u = jnp.dot(x, wu[:, cols], preferred_element_type=F32)
+            hid[:, cols] = (g / (1.0 + jnp.exp(-g)) * u).astype(BF16)
+
+        if s == 0 and c == 1:
+            weights[2].wait()
+        meta = xv[c, :, d:].astype(F32)
+        lane = lax.broadcasted_iota(jnp.int32, meta.shape, 1)
+        mine = (lane == l) | (lane == l + 8)
+        scale = jnp.sum(jnp.where(mine, meta, 0.0), axis=1, keepdims=True)
+        if s >= 2:
+            if c:
+                sent(s - 2, PART_S)
+            else:
+                sent(s - 2, DIAG_X, DIAG_Y, SUM_X, SUM_Y)
+                if s > 2:
+                    sent(s - 2, HOME)
+                else:
+                    last.wait()
+
+        @pl.loop(0, d // 512)
+        def _(i):
+            cols = pl.ds(pl.multiple_of(i * 512, 512), 512)
+            y = jnp.dot(hid[...], wd[:, cols], preferred_element_type=F32)
+            target[s % 2, :, cols] = (scale * y).astype(BF16)
+
+        if c:
+            start(s, PART_S)
+
+    def add(s, r, others, at=0, size=rows):
+        @pl.loop(0, size // 16)
+        def _(i):
+            off = pl.multiple_of(i * 16, 16)
+            here = pl.ds(r * rows + at + off, 16)
+            total = ykeep[s % 2, here, :].astype(F32)
+            for ref, base in others:
+                total += ref[s, pl.ds(base + off, 16), :].astype(F32)
+            ykeep[s % 2, here, :] = total.astype(BF16)
+
+    def reduce_diagonal(s):
+        arrived(s, PART_S)
+        add(s, 3, [(sib, 3 * rows)])
+        start(s, DIAG_X, DIAG_Y)
+
+    def reduce_sides(s):
+        arrived(s, DIAG_Y)
+        add(s, 1, [(sib, rows)], 0, half)
+        add(s, 1, [(sib, rows + half), (dg, half)], half, half)
+        start(s, SUM_X)
+        arrived(s, DIAG_X)
+        add(s, 2, [(sib, 2 * rows), (dg, 0)], 0, half)
+        add(s, 2, [(sib, 2 * rows + half)], half, half)
+        start(s, SUM_Y)
+
+    def reduce_home(s):
+        arrived(s, SUM_X, SUM_Y)
+        add(s, 0, [(sib, 0), (rx, 0), (ry, 0)])
+        if s:
+            start(s, HOME)
+        else:
+            last.start()
+
+    for s in range(1, n):
+        start(s, NODE)
+    for w in weights:
+        w.start()
+
+    gather_own(0)
+    gather_forward(0)
+    if n > 1:
+        gather_own(1)
+    gather_diagonal(0)
+    load(0)
+    for s in range(n):
+        expert(s, 1)
+        if s + 1 < n:
+            gather_forward(s + 1)
+        if s + 2 < n:
+            gather_own(s + 2)
+        if s:
+            reduce_sides(s - 1)
+        expert(s, 0)
+        if s + 1 < n:
+            gather_diagonal(s + 1)
+        reduce_diagonal(s)
+        if s + 1 < n:
+            load(s + 1)
+        if s:
+            reduce_home(s - 1)
+    reduce_sides(n - 1)
+    reduce_home(n - 1)
+
+    for s in range(1, n):
+        arrived(s, HOME)
+    for s, k in sends:
+        sent(s, k)
+    for s in range(max(0, n - 2), n):
+        sent(s, PART_S, DIAG_X, DIAG_Y, SUM_X, SUM_Y)
+        if s:
+            sent(s, HOME)
+        else:
+            last.wait()
+
+
+def on_device_fused(tokens, group_ids, local_ids, router, w_gate, w_up, w_down):
+    tok_dev, d = tokens.shape
+    ff = w_gate.shape[2]
+    n = lax.axis_size("node")
+    local_size = lax.axis_size("local")
+    group_count = group_ids.shape[1]
+    per_group = local_ids.shape[1] // group_count
+    rows = group_count * tok_dev // n
+    z = lax.axis_index("node")
+
+    affinity = jax.nn.sigmoid(jnp.dot(tokens, router, preferred_element_type=F32))
+    expert_ids = jnp.repeat(group_ids, per_group, axis=1) * local_size + local_ids
+    experts = jnp.arange(router.shape[1], dtype=jnp.int32)
+    picked = jnp.sum(
+        jnp.where(expert_ids[:, :, None] == experts, affinity[:, None, :], 0.0), axis=2
+    )
+    gate = 2.5 * picked / jnp.sum(picked, axis=1, keepdims=True)
+    lanes = jnp.arange(local_size, dtype=jnp.int32)
+    spread = jnp.sum(
+        jnp.where(
+            local_ids.reshape(tok_dev, group_count, per_group)[..., None] == lanes,
+            gate.reshape(tok_dev, group_count, per_group)[..., None],
+            0.0,
+        ),
+        axis=2,
+    )
+    high = lax.reduce_precision(spread, 8, 7)
+    low = spread - high
+    meta = jnp.concatenate(
+        [high, low, jnp.zeros((tok_dev, group_count, META - 2 * local_size), F32)], axis=2
+    ).astype(BF16)
+
+    slots = []
+    total = group_count * tok_dev
+    before = jnp.tril(jnp.ones((tok_dev, tok_dev), BF16), -1)
+    named = jnp.sum(
+        (group_ids[:, :, None] == jnp.arange(n, dtype=jnp.int32)).astype(jnp.int32), axis=1
+    )
+    earlier = jnp.dot(before, named.astype(BF16), preferred_element_type=F32).astype(jnp.int32)
+    place = jnp.sum(
+        jnp.where(group_ids[:, :, None] == jnp.arange(n, dtype=jnp.int32), earlier[:, None, :], 0),
+        axis=2,
+    )
+    slots = (z - group_ids + n) % n * rows + place
+    picks = [
+        (slots[None, :, j] == jnp.arange(total, dtype=jnp.int32)[:, None]).astype(BF16)
+        for j in range(group_count)
+    ]
+    body = jnp.dot(sum(picks), tokens, preferred_element_type=F32)
+    tail = sum(
+        jnp.dot(picks[j], meta[:, j], preferred_element_type=F32) for j in range(group_count)
+    )
+    outgoing = jnp.concatenate([body.astype(BF16), tail.astype(BF16)], axis=1)
+    outgoing = outgoing.reshape(n, rows, d + META)
+
+    wide = local_size // 2 * rows
+    any_spec = pl.BlockSpec(memory_space=pl.ANY)
+    home, _ = pl.pallas_call(
+        functools.partial(layer_kernel, n, rows, d, ff),
+        out_shape=(
+            jax.ShapeDtypeStruct((n, rows, d), BF16),
+            jax.ShapeDtypeStruct((n, 2, wide, d + META), BF16),
+        ),
+        in_specs=[any_spec] * 4,
+        out_specs=(any_spec, any_spec),
+        scratch_shapes=[
+            pltpu.VMEM((d, ff), BF16),
+            pltpu.VMEM((d, ff), BF16),
+            pltpu.VMEM((ff, d), BF16),
+            pltpu.VMEM((2, wide, d + META), BF16),
+            pltpu.VMEM((wide, ff), BF16),
+            pltpu.VMEM((2, wide, d), BF16),
+            pltpu.VMEM((2, wide, d), BF16),
+            pltpu.VMEM((n, wide, d), BF16),
+            pltpu.VMEM((n, rows, d), BF16),
+            pltpu.VMEM((n, rows, d), BF16),
+            pltpu.VMEM((n, rows, d), BF16),
+            pltpu.SemaphoreType.DMA((n, 15)),
+            pltpu.SemaphoreType.DMA((n, 15)),
+            pltpu.SemaphoreType.DMA((3,)),
+            pltpu.SemaphoreType.DMA((2,)),
+            pltpu.SemaphoreType.DMA((2,)),
+        ],
+        compiler_params=pltpu.CompilerParams(
+            collective_id=0, has_side_effects=True, vmem_limit_bytes=60 * 2**20
+        ),
+        cost_estimate=pl.CostEstimate(
+            flops=6 * n * 2 * wide * d * ff, bytes_accessed=40 * 2**20, transcendentals=0
+        ),
+    )(outgoing, w_gate[0], w_up[0], w_down[0])
+    mixed = jnp.dot(sum(picks).T, home.reshape(total, d), preferred_element_type=F32)
+    return mixed.astype(BF16)
 
 
 def solution(mesh):
+    fused = mesh.shape["local"] == 8
     return jax.shard_map(
-        on_device,
+        on_device_fused if fused else on_device_general,
         mesh=mesh,
         in_specs=(
             P(("node", "local"), None),

time: 485 us -> 180 us (0.37)
  waiting for transfers between devices: 196 us -> 0 us
  Pallas kernels: 0 us -> 169 us
  blocking collectives: 107 us -> 0 us
  local copies, waits for them, and re-layouts: 88.6 us -> 0.35 us
  matrix products: 41.6 us -> 5.36 us
  other arithmetic: 27.8 us -> 5.09 us
  starting transfers between devices: 21.9 us -> 0 us
    all_to_all x4 -> x0, waiting for transfers between devices: 196 us -> none  [the longest x1 92.3 us: on_device(): lax.all_to_all(produced, 'local', split_axis=0, concat_axis=0, tiled=True)]
    pallas_call x0 -> x1, Pallas kernels: none -> 169 us  [on_device_fused(): pl.pallas_call(functools.partial(layer_kernel, n, rows, d, ff), out_shape...]
    all_to_all x1 -> x0, blocking collectives: 107 us -> none  [on_device(): lax.all_to_all(relay_send, 'local', split_axis=0, concat_axis=0, tiled=True)]
    gather x13 -> x0, local copies, waits for them, and re-layouts: 53.1 us -> none  [the longest x1 18.6 us: on_device(): relay_back.reshape(-1, feat_width)[relay_slot]]
    dot_general x5 -> x6, matrix products: 41.6 us -> 5.36 us  [the longest x1 2.88 us: on_device_fused(): jnp.dot(sum(picks).T, home.reshape(total, d), preferred_element_type=F32)]
    all_to_all x4 -> x0, starting transfers between devices: 21.9 us -> none  [the longest x1 6.32 us: on_device(): lax.all_to_all(outgoing_ids, 'node', split_axis=0, concat_axis=0, tiled=T...]
    reduce_sum x5 -> x4, other arithmetic: 20.8 us -> 2.22 us  [the longest x1 0.76 us: on_device_fused(): jnp.sum((group_ids[:, :, None] == jnp.arange(n, dtype=jnp.int32)).astype(...]
    convert_element_type x1 -> x0, local copies, waits for them, and re-layouts: 13.9 us -> none  [on_device(): relay_terms.astype(jnp.float32)]
  transfers between devices with their start and end apart: 4 -> 0, of which waited for: 3 -> 0; matrix products, arithmetic and copies ran while one was open for 7% -> 0% of each run, Pallas kernels for 0% -> 0%
where the time goes in v1:
time: 180 us
  Pallas kernels  169 us (94%)
  matrix products  5.36 us (3%)
  other arithmetic  5.09 us (3%)
    pallas_call x1, Pallas kernels, on_device_fused(): pl.pallas_call(functools.partial(layer_kernel, n, rows, d, ff), out_shape...  169 us

profile of v1, /device:TPU:0, one launch (start us, length us, event | category | flops | bytes accessed | tf_op | source)
XLA Modules:
  0.0 179.8 jit_solution(4066009248127783547)
XLA Ops:
  0.0 0.0 copy-start
  0.0 0.1 pad.4.clone
  0.1 0.8 convert_reduce_fusion
  0.8 0.2 convolution_convert_fusion.2
  1.0 0.7 select_reduce_fusion.3
  1.8 0.7 broadcast_multiply_fusion.1
  2.5 0.7 add.44
  3.2 0.0 copy-done
  3.2 1.3 fusion.3
  4.5 0.1 select_reduce_fusion
  4.6 0.7 select_reduce_fusion.2
  5.3 0.1 copy.23
  5.4 0.1 copy.24
  5.6 0.1 maximum_maximum_fusion
  5.7 0.1 fusion.5
  5.8 0.2 fusion
  6.0 0.6 convolution_convert_fusion
  6.6 1.4 pad_maximum_fusion
  8.0 168.9 %shard_map.73 = (bf16[4,64,3584]{2,1,0:T(8,128)(2,1)}, bf16[4,2,256,3712]{3,2,1,0:T(8,128)(2,1)}) custom-call(bf16[4,64,3712]{2,1,0:T(8,128)(2,1)} %bitcast.22, bf16[3584,1024]{1,0:T(8,128)(2,1)} %bitcast.27, bf16[3584,1024]{1,0:T(8,128)(2,1)} %bitcast.28, bf16[1024,3584]{1,0:T(8,128)(2,1)} %bitcast.29), custom_call_target="tpu_custom_call" | custom-call | flops 45097156608 | bytes 41943040 | tf_op jit(solution)/shard_map/pallas_call | solution.py:375
  176.9 2.9 %convolution_convert_fusion.1 = bf16[128,3584]{1,0:T(8,128)(2,1)} fusion(bf16[256,3584]{1,0:T(8,128)(2,1)} %bitcast.23, s32[128]{0:T(128)S(1)} %get-tuple-element.11, s32[128]{0:T(128)S(1)} %get-tuple-element.12), kind=kOutput, calls=%fused_computation.1 | convolution fusion | flops 235601920 | bytes 2753536 | tf_op jit(solution)/shard_map/dot_general | solution.py:408
  (7 shorter events, 0.0 us)
Async XLA Ops:
  0.0 3.2 %copy-start = (bf16[128,3584]{1,0:T(8,128)(2,1)S(1)}, bf16[128,3584]{1,0:T(8,128)(2,1)}, u32[]{:S(2)}) copy-start(bf16[128,3584]{1,0:T(8,128)(2,1)} %param.7) | copy-start | bytes 2752516

commit v2 on v1

--- a/solution.py
+++ b/solution.py
@@ -98,7 +98,7 @@
     return mixed.astype(BF16)
 
 
-OWN_X, OWN_Y, OWN_S, FWD_Y, FWD_X, SIB_X, SIB_Y, SIB_D, PART_S, DIAG_X, DIAG_Y, SUM_X, SUM_Y, HOME, NODE = range(15)
+OWN_X, OWN_Y, OWN_S, FWD_Y, FWD_X, SIB_X, SIB_Y, SIB_D, PART_S, DIAG_X, DIAG_Y, SUM_X, SUM_Y, HOME, NODE, EARLY_X, EARLY_Y = range(17)
 
 
 def layer_kernel(
@@ -156,8 +156,10 @@
         cp[s, PART_S] = copy(s, PART_S, ysend.at[s % 2], sib.at[s], sibling)
         cp[s, DIAG_X] = copy(s, DIAG_X, kp(s, 3, 0, half), dg.at[s, pl.ds(0, half)], xn)
         cp[s, DIAG_Y] = copy(s, DIAG_Y, kp(s, 3, half, half), dg.at[s, pl.ds(half, half)], yn)
-        cp[s, SUM_X] = copy(s, SUM_X, kp(s, 1), rx.at[s], xn)
-        cp[s, SUM_Y] = copy(s, SUM_Y, kp(s, 2), ry.at[s], yn)
+        cp[s, SUM_X] = copy(s, SUM_X, kp(s, 1, half, half), rx.at[s, pl.ds(half, half)], xn)
+        cp[s, EARLY_X] = copy(s, EARLY_X, kp(s, 1, 0, half), rx.at[s, pl.ds(0, half)], xn)
+        cp[s, SUM_Y] = copy(s, SUM_Y, kp(s, 2, 0, half), ry.at[s, pl.ds(0, half)], yn)
+        cp[s, EARLY_Y] = copy(s, EARLY_Y, kp(s, 2, half, half), ry.at[s, pl.ds(half, half)], yn)
         if s:
             cp[s, HOME] = copy(s, HOME, kp(s, 0), home.at[s], (lax.rem(z + s, n), l))
             cp[s, NODE] = copy(s, NODE, out_ref.at[s], blk(s, 0, 0), (lax.rem(z - s + n, n), l))
@@ -167,7 +169,7 @@
     def start(s, *kinds):
         for k in kinds:
             cp[s, k].start()
-            if k not in (PART_S, DIAG_X, DIAG_Y, SUM_X, SUM_Y, HOME):
+            if k not in (PART_S, DIAG_X, DIAG_Y, SUM_X, SUM_Y, EARLY_X, EARLY_Y, HOME):
                 sends.append((s, k))
 
     def arrived(s, *kinds):
@@ -225,7 +227,7 @@
             if c:
                 sent(s - 2, PART_S)
             else:
-                sent(s - 2, DIAG_X, DIAG_Y, SUM_X, SUM_Y)
+                sent(s - 2, DIAG_X, DIAG_Y, SUM_X, SUM_Y, EARLY_X, EARLY_Y)
                 if s > 2:
                     sent(s - 2, HOME)
                 else:
@@ -254,19 +256,21 @@
         arrived(s, PART_S)
         add(s, 3, [(sib, 3 * rows)])
         start(s, DIAG_X, DIAG_Y)
+        add(s, 1, [(sib, rows)], 0, half)
+        start(s, EARLY_X)
+        add(s, 2, [(sib, 2 * rows + half)], half, half)
+        start(s, EARLY_Y)
 
     def reduce_sides(s):
         arrived(s, DIAG_Y)
-        add(s, 1, [(sib, rows)], 0, half)
         add(s, 1, [(sib, rows + half), (dg, half)], half, half)
         start(s, SUM_X)
         arrived(s, DIAG_X)
         add(s, 2, [(sib, 2 * rows), (dg, 0)], 0, half)
-        add(s, 2, [(sib, 2 * rows + half)], half, half)
         start(s, SUM_Y)
 
     def reduce_home(s):
-        arrived(s, SUM_X, SUM_Y)
+        arrived(s, SUM_X, SUM_Y, EARLY_X, EARLY_Y)
         add(s, 0, [(sib, 0), (rx, 0), (ry, 0)])
         if s:
             start(s, HOME)
@@ -288,14 +292,16 @@
         expert(s, 1)
         if s + 1 < n:
             gather_forward(s + 1)
-        if s + 2 < n:
-            gather_own(s + 2)
+        if s == 0 and n > 2:
+            gather_own(2)
         if s:
             reduce_sides(s - 1)
         expert(s, 0)
         if s + 1 < n:
             gather_diagonal(s + 1)
         reduce_diagonal(s)
+        if s + 3 < n:
+            gather_own(s + 3)
         if s + 1 < n:
             load(s + 1)
         if s:
@@ -308,7 +314,7 @@
     for s, k in sends:
         sent(s, k)
     for s in range(max(0, n - 2), n):
-        sent(s, PART_S, DIAG_X, DIAG_Y, SUM_X, SUM_Y)
+        sent(s, PART_S, DIAG_X, DIAG_Y, SUM_X, SUM_Y, EARLY_X, EARLY_Y)
         if s:
             sent(s, HOME)
         else:
@@ -392,8 +398,8 @@
             pltpu.VMEM((n, rows, d), BF16),
             pltpu.VMEM((n, rows, d), BF16),
             pltpu.VMEM((n, rows, d), BF16),
-            pltpu.SemaphoreType.DMA((n, 15)),
-            pltpu.SemaphoreType.DMA((n, 15)),
+            pltpu.SemaphoreType.DMA((n, 17)),
+            pltpu.SemaphoreType.DMA((n, 17)),
             pltpu.SemaphoreType.DMA((3,)),
             pltpu.SemaphoreType.DMA((2,)),
             pltpu.SemaphoreType.DMA((2,)),

time: 180 us -> 179 us (level)
  no operation moved by 1% of the time
where the time goes in v2:
time: 179 us
  Pallas kernels  168 us (94%)
  matrix products  5.35 us (3%)
  other arithmetic  5.09 us (3%)
    pallas_call x1, Pallas kernels, on_device_fused(): pl.pallas_call(functools.partial(layer_kernel, n, rows, d, ff), out_shape...  168 us

profile of v2, /device:TPU:0, one launch (start us, length us, event | category | flops | bytes accessed | tf_op | source)
XLA Modules:
  0.0 178.9 jit_solution(8255851982985842644)
XLA Ops:
  0.0 0.0 copy-start
  0.0 0.1 pad.4.clone
  0.1 0.8 convert_reduce_fusion
  0.8 0.2 convolution_convert_fusion.2
  1.0 0.7 select_reduce_fusion.3
  1.8 0.7 broadcast_multiply_fusion.1
  2.5 0.7 add.44
  3.2 0.0 copy-done
  3.2 1.3 fusion.3
  4.5 0.1 select_reduce_fusion
  4.6 0.7 select_reduce_fusion.2
  5.3 0.1 copy.23
  5.4 0.1 copy.24
  5.6 0.1 maximum_maximum_fusion
  5.7 0.1 fusion.5
  5.8 0.2 fusion
  6.0 0.6 convolution_convert_fusion
  6.6 1.4 pad_maximum_fusion
  8.0 168.1 %shard_map.73 = (bf16[4,64,3584]{2,1,0:T(8,128)(2,1)}, bf16[4,2,256,3712]{3,2,1,0:T(8,128)(2,1)}) custom-call(bf16[4,64,3712]{2,1,0:T(8,128)(2,1)} %bitcast.22, bf16[3584,1024]{1,0:T(8,128)(2,1)} %bitcast.27, bf16[3584,1024]{1,0:T(8,128)(2,1)} %bitcast.28, bf16[1024,3584]{1,0:T(8,128)(2,1)} %bitcast.29), custom_call_target="tpu_custom_call" | custom-call | flops 45097156608 | bytes 41943040 | tf_op jit(solution)/shard_map/pallas_call | solution.py:381
  176.1 2.9 %convolution_convert_fusion.1 = bf16[128,3584]{1,0:T(8,128)(2,1)} fusion(bf16[256,3584]{1,0:T(8,128)(2,1)} %bitcast.23, s32[128]{0:T(128)S(1)} %get-tuple-element.11, s32[128]{0:T(128)S(1)} %get-tuple-element.12), kind=kOutput, calls=%fused_computation.1 | convolution fusion | flops 235601920 | bytes 2753536 | tf_op jit(solution)/shard_map/dot_general | solution.py:414
  (7 shorter events, 0.0 us)
Async XLA Ops:
  0.0 3.2 %copy-start = (bf16[128,3584]{1,0:T(8,128)(2,1)S(1)}, bf16[128,3584]{1,0:T(8,128)(2,1)}, u32[]{:S(2)}) copy-start(bf16[128,3584]{1,0:T(8,128)(2,1)} %param.7) | copy-start | bytes 2752516
